TPU v7x, 32 devices: a whole 2x2x4 slice. The times are simulated.
32 devices in a mesh: dp: 4 (over x, core), segment: 2 (over y), seq: 4 (over z).
Axes of the slice: x: 2, y: 2, z: 4, core: 2. Of those that a mesh axis runs over, the one named last changes fastest.
Arguments:
- activations: bfloat16 [4, 4, 512, 768], P('dp', None, 'seq'), may hold values from -6 to 6
- conv_weight: bfloat16 [2, 5, 768, 768], P('segment', None, ('dp', 'seq')), may hold values from -0.125 to 0.125
- norm_gain: float32 [2, 768], P('segment'), may hold values from 0.25 to 1.75
- conv_bias: float32 [2, 768], P('segment'), may hold values from -3 to 3
Outputs:
- block_outputs: bfloat16 [2, 4, 4, 512, 768], P('segment', 'dp', None, 'seq')
All inputs are finite; a program needn't handle non-finite values.
Results may differ from a plain program's by a relative error of at most 0.0065.
Values may be sent and summed in bfloat16 or wider, within the bound.
A program may use at most 64 MiB of HBM per device.

v0:
```python
import jax
import jax.numpy as jnp
from jax import lax
from jax.sharding import PartitionSpec as P


def extended(cells, sides, width):
    for axis, dim in sides:
        count = lax.axis_size(axis)
        ends = count - 1
        head = lax.slice_in_dim(cells, 0, width, axis=dim)
        tail = lax.slice_in_dim(cells, cells.shape[dim] - width, cells.shape[dim], axis=dim)
        cells = jnp.concatenate(
            [
                lax.ppermute(tail, axis, [(i, (i + 1) % count) for i in range(ends)]),
                cells,
                lax.ppermute(head, axis, [((i + 1) % count, i) for i in range(ends)]),
            ],
            axis=dim,
        )
    return cells


def from_behind(block, axis, distance):
    devices = range(lax.axis_size(axis))
    route = [(i - distance, i) for i in devices if i - distance in devices]
    return lax.ppermute(block, axis, route)


def per_device(activations, conv_weight, norm_gain, conv_bias):
    kernel = lax.all_gather(conv_weight, ("dp", "seq"), axis=2, tiled=True)[0]
    gain = norm_gain[0]
    bias = conv_bias[0]
    inputs = activations[0]
    micro_count = inputs.shape[0]
    rows = inputs.shape[1]
    width = inputs.shape[2]
    segments = lax.axis_size("segment")
    segment = lax.axis_index("segment")
    turns = segments + micro_count - 1
    taps = kernel.shape[0]

    def convolve(padded):
        total = jnp.zeros((rows, width), jnp.float32)
        for tap in range(taps):
            total = total + jnp.dot(
                padded[tap : tap + rows], kernel[tap], preferred_element_type=jnp.float32
            )
        return total

    def skipped(padded):
        return jnp.zeros((rows, width), jnp.float32)

    def turn(step, carry):
        incoming, results, joined = carry
        micro = step - segment
        valid = jnp.logical_and(micro >= 0, micro < micro_count)
        picked = jnp.clip(micro, 0, micro_count - 1)
        own = lax.dynamic_index_in_dim(inputs, picked, 0, keepdims=False)
        current = jnp.where(segment == 0, own, incoming)
        wide = current.astype(jnp.float32)
        stat = jnp.mean(wide * wide, axis=-1, keepdims=True)
        normed = (wide / jnp.sqrt(stat + 1e-06) * gain).astype(jnp.bfloat16)
        padded = extended(normed, (("seq", 0),), 2)
        total = lax.cond(valid, convolve, skipped, padded)
        lifted = wide + jax.nn.gelu(total + bias, approximate=True)
        sent = lifted.astype(jnp.bfloat16)
        stored = lax.dynamic_update_index_in_dim(results, lifted, picked, 0)
        results = jnp.where(valid, stored, results)
        following = from_behind(sent, "segment", 1)
        return (following, results, joined)

    start = (
        jnp.zeros((rows, width), jnp.bfloat16),
        jnp.zeros((micro_count, rows, width), jnp.float32),
        jnp.zeros((micro_count, rows, width), jnp.bfloat16),
    )
    incoming, results, joined = lax.fori_loop(0, turns, turn, start)
    rounded = results.astype(jnp.bfloat16)
    joined = from_behind(rounded, "segment", segments - 1)
    final = (results + joined.astype(jnp.float32)).astype(jnp.bfloat16)
    output = jnp.where(segment == segments - 1, final, rounded)
    return output[None, None]


def solution(mesh):
    in_specs = (
        P("dp", None, "seq", None),
        P("segment", None, ("dp", "seq"), None),
        P("segment", None),
        P("segment", None),
    )
    out_specs = P("segment", "dp", None, "seq", None)
    return jax.shard_map(
        per_device, mesh=mesh, in_specs=in_specs, out_specs=out_specs, check_vma=False
    )
```

profile of v0, /device:TPU:28, one launch (start us, length us, event | category | flops | bytes accessed | tf_op | source)
XLA Modules:
  0.0 217.0 jit_solution(3128577337960555985)
XLA Ops:
  7.3 61.8 %all-gather.2.cloned.1.call-done = bf16[1,5,768,768]{3,2,1,0:T(8,128)(2,1)} async-done(((bf16[1,5,48,768]{3,2,1,0:T(8,128)(2,1)}), bf16[1,5,768,768]{3,2,1,0:T(8,128)(2,1)}) %all-gather.2.cloned.1.call-update) | async-done | bytes 5898256 | tf_op jit(solution)/shard_map/all_gather | solution.py:31
  69.2 126.0 %while.16 = (s32[]{:T(128)}, bf16[128,768]{1,0:T(8,128)(2,1)S(1)}, f32[4,128,768]{2,1,0:T(8,128)S(1)}, pred[]{:T(512)}, s32[]{:T(128)}, /*index=5*/bf16[4,128,76...) while((s32[]{:T(128)}, bf16[128,768]{1,0:T(8,128)(2,1)S(1)}, ...), condition=%wide.region_4.5_spmd, body=%wide.region_0.4_spmd.sunk | while | flops 759122048 | bytes 14819693 | solution.py:78
  70.5 3.4 %collective-permute-start = (bf16[2,768]{1,0:T(2,128)(2,1)S(1)}, bf16[2,768]{1,0:T(2,128)(2,1)S(1)}, u32[]{:S(2)}, u32[]{:S(2)}) collective-permute-start(bf16[2,768]{1,0:T(2,128)(2,1)S(1)} %get-tuple-element.282), channel_id=1, source_target_pairs={{1,0},{2,1},{3,2},{5,4},{6,5},{7,6},{9,8},{10,9},{11,10},{13,12},{... | collective-permute-start | bytes 9224 | tf_op jit(solution)/shard_map/while/body/eval_jaxpr/ppermute | solution.py:17
  75.2 4.1 %collective-permute-done.1 = bf16[2,768]{1,0:T(2,128)(2,1)S(1)} collective-permute-done((bf16[2,768]{1,0:T(2,128)(2,1)S(1)}, bf16[2,768]{1,0:T(2,128)(2,1)S(1)}, u32[]{:S(2)}, u32[]{:S(2)}) %collective-permute-start.1) | collective-permute-done | bytes 3104 | tf_op jit(solution)/shard_map/while/body/eval_jaxpr/ppermute | solution.py:15
  81.2 12.2 %collective-permute-done.2 = bf16[128,768]{1,0:T(8,128)(2,1)S(1)} collective-permute-done((bf16[128,768]{1,0:T(8,128)(2,1)S(1)}, bf16[128,768]{1,0:T(8,128)(2,1)S(1)}, u32[]{:S(2)}, u32[]{:S(2)}) %collective-permute-start.2) | collective-permute-done | bytes 196640 | tf_op jit(solution)/shard_map/while/body/eval_jaxpr/ppermute | solution.py:27
  94.6 2.9 %collective-permute-start = (bf16[2,768]{1,0:T(2,128)(2,1)S(1)}, bf16[2,768]{1,0:T(2,128)(2,1)S(1)}, u32[]{:S(2)}, u32[]{:S(2)}) collective-permute-start(bf16[2,768]{1,0:T(2,128)(2,1)S(1)} %get-tuple-element.282), channel_id=1, source_target_pairs={{1,0},{2,1},{3,2},{5,4},{6,5},{7,6},{9,8},{10,9},{11,10},{13,12},{... | collective-permute-start | bytes 9224 | tf_op jit(solution)/shard_map/while/body/eval_jaxpr/ppermute | solution.py:17
  98.9 4.1 %collective-permute-done.1 = bf16[2,768]{1,0:T(2,128)(2,1)S(1)} collective-permute-done((bf16[2,768]{1,0:T(2,128)(2,1)S(1)}, bf16[2,768]{1,0:T(2,128)(2,1)S(1)}, u32[]{:S(2)}, u32[]{:S(2)}) %collective-permute-start.1) | collective-permute-done | bytes 3104 | tf_op jit(solution)/shard_map/while/body/eval_jaxpr/ppermute | solution.py:15
  103.1 8.0 %conditional.2 = (f32[128,768]{1,0:T(8,128)S(1)}) conditional(s32[]{:T(128)} %convert_element_type.83, () %tuple.46, (bf16[132,768]{1,0:T(8,128)(2,1)S(1)}, bf16[5,768,768]{2,1,0:T(8,128)(2,1)}, bf16[128,768]{1,0:T(8,128)(2,1)S(1)}) %tuple.47), branch_computations={%region_2.2_spmd, %region_3.3_spmd} | conditional | flops 755367936 | bytes 10420232 | solution.py:65
  112.9 6.1 %collective-permute-done.2 = bf16[128,768]{1,0:T(8,128)(2,1)S(1)} collective-permute-done((bf16[128,768]{1,0:T(8,128)(2,1)S(1)}, bf16[128,768]{1,0:T(8,128)(2,1)S(1)}, u32[]{:S(2)}, u32[]{:S(2)}) %collective-permute-start.2) | collective-permute-done | bytes 196640 | tf_op jit(solution)/shard_map/while/body/eval_jaxpr/ppermute | solution.py:27
  120.2 2.4 %collective-permute-start = (bf16[2,768]{1,0:T(2,128)(2,1)S(1)}, bf16[2,768]{1,0:T(2,128)(2,1)S(1)}, u32[]{:S(2)}, u32[]{:S(2)}) collective-permute-start(bf16[2,768]{1,0:T(2,128)(2,1)S(1)} %get-tuple-element.282), channel_id=1, source_target_pairs={{1,0},{2,1},{3,2},{5,4},{6,5},{7,6},{9,8},{10,9},{11,10},{13,12},{... | collective-permute-start | bytes 9224 | tf_op jit(solution)/shard_map/while/body/eval_jaxpr/ppermute | solution.py:17
  123.9 4.1 %collective-permute-done.1 = bf16[2,768]{1,0:T(2,128)(2,1)S(1)} collective-permute-done((bf16[2,768]{1,0:T(2,128)(2,1)S(1)}, bf16[2,768]{1,0:T(2,128)(2,1)S(1)}, u32[]{:S(2)}, u32[]{:S(2)}) %collective-permute-start.1) | collective-permute-done | bytes 3104 | tf_op jit(solution)/shard_map/while/body/eval_jaxpr/ppermute | solution.py:15
  128.1 8.0 %conditional.2 = (f32[128,768]{1,0:T(8,128)S(1)}) conditional(s32[]{:T(128)} %convert_element_type.83, () %tuple.46, (bf16[132,768]{1,0:T(8,128)(2,1)S(1)}, bf16[5,768,768]{2,1,0:T(8,128)(2,1)}, bf16[128,768]{1,0:T(8,128)(2,1)S(1)}) %tuple.47), branch_computations={%region_2.2_spmd, %region_3.3_spmd} | conditional | flops 755367936 | bytes 10420232 | solution.py:65
  134.6 1.6 convolution_add_fusion
  137.9 6.1 %collective-permute-done.2 = bf16[128,768]{1,0:T(8,128)(2,1)S(1)} collective-permute-done((bf16[128,768]{1,0:T(8,128)(2,1)S(1)}, bf16[128,768]{1,0:T(8,128)(2,1)S(1)}, u32[]{:S(2)}, u32[]{:S(2)}) %collective-permute-start.2) | collective-permute-done | bytes 196640 | tf_op jit(solution)/shard_map/while/body/eval_jaxpr/ppermute | solution.py:27
  145.2 1.9 collective-permute-start
  148.5 4.1 %collective-permute-done.1 = bf16[2,768]{1,0:T(2,128)(2,1)S(1)} collective-permute-done((bf16[2,768]{1,0:T(2,128)(2,1)S(1)}, bf16[2,768]{1,0:T(2,128)(2,1)S(1)}, u32[]{:S(2)}, u32[]{:S(2)}) %collective-permute-start.1) | collective-permute-done | bytes 3104 | tf_op jit(solution)/shard_map/while/body/eval_jaxpr/ppermute | solution.py:15
  152.7 8.0 %conditional.2 = (f32[128,768]{1,0:T(8,128)S(1)}) conditional(s32[]{:T(128)} %convert_element_type.83, () %tuple.46, (bf16[132,768]{1,0:T(8,128)(2,1)S(1)}, bf16[5,768,768]{2,1,0:T(8,128)(2,1)}, bf16[128,768]{1,0:T(8,128)(2,1)S(1)}) %tuple.47), branch_computations={%region_2.2_spmd, %region_3.3_spmd} | conditional | flops 755367936 | bytes 10420232 | solution.py:65
  162.4 6.1 %collective-permute-done.2 = bf16[128,768]{1,0:T(8,128)(2,1)S(1)} collective-permute-done((bf16[128,768]{1,0:T(8,128)(2,1)S(1)}, bf16[128,768]{1,0:T(8,128)(2,1)S(1)}, u32[]{:S(2)}, u32[]{:S(2)}) %collective-permute-start.2) | collective-permute-done | bytes 196640 | tf_op jit(solution)/shard_map/while/body/eval_jaxpr/ppermute | solution.py:27
  169.7 1.9 collective-permute-start
  173.0 4.1 %collective-permute-done.1 = bf16[2,768]{1,0:T(2,128)(2,1)S(1)} collective-permute-done((bf16[2,768]{1,0:T(2,128)(2,1)S(1)}, bf16[2,768]{1,0:T(2,128)(2,1)S(1)}, u32[]{:S(2)}, u32[]{:S(2)}) %collective-permute-start.1) | collective-permute-done | bytes 3104 | tf_op jit(solution)/shard_map/while/body/eval_jaxpr/ppermute | solution.py:15
  177.2 8.0 %conditional.2 = (f32[128,768]{1,0:T(8,128)S(1)}) conditional(s32[]{:T(128)} %convert_element_type.83, () %tuple.46, (bf16[132,768]{1,0:T(8,128)(2,1)S(1)}, bf16[5,768,768]{2,1,0:T(8,128)(2,1)}, bf16[128,768]{1,0:T(8,128)(2,1)S(1)}) %tuple.47), branch_computations={%region_2.2_spmd, %region_3.3_spmd} | conditional | flops 755367936 | bytes 10420232 | solution.py:65
  183.6 1.6 convolution_add_fusion
  186.9 8.2 %collective-permute-done.2 = bf16[128,768]{1,0:T(8,128)(2,1)S(1)} collective-permute-done((bf16[128,768]{1,0:T(8,128)(2,1)S(1)}, bf16[128,768]{1,0:T(8,128)(2,1)S(1)}, u32[]{:S(2)}, u32[]{:S(2)}) %collective-permute-start.2) | collective-permute-done | bytes 196640 | tf_op jit(solution)/shard_map/while/body/eval_jaxpr/ppermute | solution.py:27
  196.5 12.6 %collective-permute-done.3 = bf16[4,128,768]{2,1,0:T(8,128)(2,1)S(1)} collective-permute-done((bf16[4,128,768]{2,1,0:T(8,128)(2,1)S(1)}, bf16[4,128,768]{2,1,0:T(8,128)(2,1)S(1)}, u32[]{:S(2)}, u32[]{:S(2)}) %collective-permute-start.3) | collective-permute-done | bytes 786464 | tf_op jit(solution)/shard_map/ppermute | solution.py:27
  (91 shorter events, 53.4 us)
Async XLA Ops:
  6.5 62.6 %copy-start = (f32[1,768]{1,0:T(1,128)S(1)}, f32[1,768]{1,0:T(1,128)}, u32[]{:S(2)}) copy-start(f32[1,768]{1,0:T(1,128)} %param.10) | copy-start | bytes 9220
  6.5 62.7 %copy-start.1 = (f32[1,768]{1,0:T(1,128)S(1)}, f32[1,768]{1,0:T(1,128)}, u32[]{:S(2)}) copy-start(f32[1,768]{1,0:T(1,128)} %param.11) | copy-start | bytes 9220
  6.5 62.5 %all-gather.2.cloned.1.call-start = ((), (), s32[]{:S(2)}) async-start(), calls=%async_computation | async-start | bytes 6266880 | tf_op jit(solution)/shard_map/all_gather | solution.py:31
  70.5 4.7 %collective-permute-start = (bf16[2,768]{1,0:T(2,128)(2,1)S(1)}, bf16[2,768]{1,0:T(2,128)(2,1)S(1)}, u32[]{:S(2)}, u32[]{:S(2)}) collective-permute-start(bf16[2,768]{1,0:T(2,128)(2,1)S(1)} %get-tuple-element.282), channel_id=1, source_target_pairs={{1,0},{2,1},{3,2},{5,4},{6,5},{7,6},{9,8},{10,9},{11,10},{13,12},{... | collective-permute-start | bytes 9224 | tf_op jit(solution)/shard_map/while/body/eval_jaxpr/ppermute | solution.py:17
  73.9 5.5 %collective-permute-start.1 = (bf16[2,768]{1,0:T(2,128)(2,1)S(1)}, bf16[2,768]{1,0:T(2,128)(2,1)S(1)}, u32[]{:S(2)}, u32[]{:S(2)}) collective-permute-start(bf16[2,768]{1,0:T(2,128)(2,1)S(1)} %get-tuple-element.283), channel_id=1, source_target_pairs={{0,1},{1,2},{2,3},{4,5},{5,6},{6,7},{8,9},{9,10},{10,11},{12,13},{... | collective-permute-start | bytes 9224 | tf_op jit(solution)/shard_map/while/body/eval_jaxpr/ppermute | solution.py:15
  79.7 13.7 %collective-permute-start.2 = (bf16[128,768]{1,0:T(8,128)(2,1)S(1)}, bf16[128,768]{1,0:T(8,128)(2,1)S(1)}, u32[]{:S(2)}, u32[]{:S(2)}) collective-permute-start(bf16[128,768]{1,0:T(8,128)(2,1)S(1)} %fusion.39), channel_id=1, source_target_pairs={{0,4},{1,5},{2,6},{3,7},{8,12},{9,13},{10,14},{11,15},{16,20},{17,... | collective-permute-start | bytes 589832 | tf_op jit(solution)/shard_map/while/body/eval_jaxpr/ppermute | solution.py:27
  94.6 4.3 %collective-permute-start = (bf16[2,768]{1,0:T(2,128)(2,1)S(1)}, bf16[2,768]{1,0:T(2,128)(2,1)S(1)}, u32[]{:S(2)}, u32[]{:S(2)}) collective-permute-start(bf16[2,768]{1,0:T(2,128)(2,1)S(1)} %get-tuple-element.282), channel_id=1, source_target_pairs={{1,0},{2,1},{3,2},{5,4},{6,5},{7,6},{9,8},{10,9},{11,10},{13,12},{... | collective-permute-start | bytes 9224 | tf_op jit(solution)/shard_map/while/body/eval_jaxpr/ppermute | solution.py:17
  97.6 5.5 %collective-permute-start.1 = (bf16[2,768]{1,0:T(2,128)(2,1)S(1)}, bf16[2,768]{1,0:T(2,128)(2,1)S(1)}, u32[]{:S(2)}, u32[]{:S(2)}) collective-permute-start(bf16[2,768]{1,0:T(2,128)(2,1)S(1)} %get-tuple-element.283), channel_id=1, source_target_pairs={{0,1},{1,2},{2,3},{4,5},{5,6},{6,7},{8,9},{9,10},{10,11},{12,13},{... | collective-permute-start | bytes 9224 | tf_op jit(solution)/shard_map/while/body/eval_jaxpr/ppermute | solution.py:15
  111.3 7.6 %collective-permute-start.2 = (bf16[128,768]{1,0:T(8,128)(2,1)S(1)}, bf16[128,768]{1,0:T(8,128)(2,1)S(1)}, u32[]{:S(2)}, u32[]{:S(2)}) collective-permute-start(bf16[128,768]{1,0:T(8,128)(2,1)S(1)} %fusion.39), channel_id=1, source_target_pairs={{0,4},{1,5},{2,6},{3,7},{8,12},{9,13},{10,14},{11,15},{16,20},{17,... | collective-permute-start | bytes 589832 | tf_op jit(solution)/shard_map/while/body/eval_jaxpr/ppermute | solution.py:27
  120.2 3.8 %collective-permute-start = (bf16[2,768]{1,0:T(2,128)(2,1)S(1)}, bf16[2,768]{1,0:T(2,128)(2,1)S(1)}, u32[]{:S(2)}, u32[]{:S(2)}) collective-permute-start(bf16[2,768]{1,0:T(2,128)(2,1)S(1)} %get-tuple-element.282), channel_id=1, source_target_pairs={{1,0},{2,1},{3,2},{5,4},{6,5},{7,6},{9,8},{10,9},{11,10},{13,12},{... | collective-permute-start | bytes 9224 | tf_op jit(solution)/shard_map/while/body/eval_jaxpr/ppermute | solution.py:17
  122.6 5.5 %collective-permute-start.1 = (bf16[2,768]{1,0:T(2,128)(2,1)S(1)}, bf16[2,768]{1,0:T(2,128)(2,1)S(1)}, u32[]{:S(2)}, u32[]{:S(2)}) collective-permute-start(bf16[2,768]{1,0:T(2,128)(2,1)S(1)} %get-tuple-element.283), channel_id=1, source_target_pairs={{0,1},{1,2},{2,3},{4,5},{5,6},{6,7},{8,9},{9,10},{10,11},{12,13},{... | collective-permute-start | bytes 9224 | tf_op jit(solution)/shard_map/while/body/eval_jaxpr/ppermute | solution.py:15
  136.4 7.6 %collective-permute-start.2 = (bf16[128,768]{1,0:T(8,128)(2,1)S(1)}, bf16[128,768]{1,0:T(8,128)(2,1)S(1)}, u32[]{:S(2)}, u32[]{:S(2)}) collective-permute-start(bf16[128,768]{1,0:T(8,128)(2,1)S(1)} %fusion.39), channel_id=1, source_target_pairs={{0,4},{1,5},{2,6},{3,7},{8,12},{9,13},{10,14},{11,15},{16,20},{17,... | collective-permute-start | bytes 589832 | tf_op jit(solution)/shard_map/while/body/eval_jaxpr/ppermute | solution.py:27
  145.2 3.3 %collective-permute-start = (bf16[2,768]{1,0:T(2,128)(2,1)S(1)}, bf16[2,768]{1,0:T(2,128)(2,1)S(1)}, u32[]{:S(2)}, u32[]{:S(2)}) collective-permute-start(bf16[2,768]{1,0:T(2,128)(2,1)S(1)} %get-tuple-element.282), channel_id=1, source_target_pairs={{1,0},{2,1},{3,2},{5,4},{6,5},{7,6},{9,8},{10,9},{11,10},{13,12},{... | collective-permute-start | bytes 9224 | tf_op jit(solution)/shard_map/while/body/eval_jaxpr/ppermute | solution.py:17
  147.1 5.5 %collective-permute-start.1 = (bf16[2,768]{1,0:T(2,128)(2,1)S(1)}, bf16[2,768]{1,0:T(2,128)(2,1)S(1)}, u32[]{:S(2)}, u32[]{:S(2)}) collective-permute-start(bf16[2,768]{1,0:T(2,128)(2,1)S(1)} %get-tuple-element.283), channel_id=1, source_target_pairs={{0,1},{1,2},{2,3},{4,5},{5,6},{6,7},{8,9},{9,10},{10,11},{12,13},{... | collective-permute-start | bytes 9224 | tf_op jit(solution)/shard_map/while/body/eval_jaxpr/ppermute | solution.py:15
  160.9 7.6 %collective-permute-start.2 = (bf16[128,768]{1,0:T(8,128)(2,1)S(1)}, bf16[128,768]{1,0:T(8,128)(2,1)S(1)}, u32[]{:S(2)}, u32[]{:S(2)}) collective-permute-start(bf16[128,768]{1,0:T(8,128)(2,1)S(1)} %fusion.39), channel_id=1, source_target_pairs={{0,4},{1,5},{2,6},{3,7},{8,12},{9,13},{10,14},{11,15},{16,20},{17,... | collective-permute-start | bytes 589832 | tf_op jit(solution)/shard_map/while/body/eval_jaxpr/ppermute | solution.py:27
  169.7 3.3 %collective-permute-start = (bf16[2,768]{1,0:T(2,128)(2,1)S(1)}, bf16[2,768]{1,0:T(2,128)(2,1)S(1)}, u32[]{:S(2)}, u32[]{:S(2)}) collective-permute-start(bf16[2,768]{1,0:T(2,128)(2,1)S(1)} %get-tuple-element.282), channel_id=1, source_target_pairs={{1,0},{2,1},{3,2},{5,4},{6,5},{7,6},{9,8},{10,9},{11,10},{13,12},{... | collective-permute-start | bytes 9224 | tf_op jit(solution)/shard_map/while/body/eval_jaxpr/ppermute | solution.py:17
  171.7 5.5 %collective-permute-start.1 = (bf16[2,768]{1,0:T(2,128)(2,1)S(1)}, bf16[2,768]{1,0:T(2,128)(2,1)S(1)}, u32[]{:S(2)}, u32[]{:S(2)}) collective-permute-start(bf16[2,768]{1,0:T(2,128)(2,1)S(1)} %get-tuple-element.283), channel_id=1, source_target_pairs={{0,1},{1,2},{2,3},{4,5},{5,6},{6,7},{8,9},{9,10},{10,11},{12,13},{... | collective-permute-start | bytes 9224 | tf_op jit(solution)/shard_map/while/body/eval_jaxpr/ppermute | solution.py:15
  185.4 9.7 %collective-permute-start.2 = (bf16[128,768]{1,0:T(8,128)(2,1)S(1)}, bf16[128,768]{1,0:T(8,128)(2,1)S(1)}, u32[]{:S(2)}, u32[]{:S(2)}) collective-permute-start(bf16[128,768]{1,0:T(8,128)(2,1)S(1)} %fusion.39), channel_id=1, source_target_pairs={{0,4},{1,5},{2,6},{3,7},{8,12},{9,13},{10,14},{11,15},{16,20},{17,... | collective-permute-start | bytes 589832 | tf_op jit(solution)/shard_map/while/body/eval_jaxpr/ppermute | solution.py:27
  195.2 13.9 %collective-permute-start.3 = (bf16[4,128,768]{2,1,0:T(8,128)(2,1)S(1)}, bf16[4,128,768]{2,1,0:T(8,128)(2,1)S(1)}, u32[]{:S(2)}, u32[]{:S(2)}) collective-permute-start(bf16[4,128,768]{2,1,0:T(8,128)(2,1)S(1)} %convert_element_type.41), channel_id=1, source_target_pairs={{0,4},{1,5},{2,6},{3,7},{8,12},{9,13},{10,14},{11,15},{16,20},{17,... | collective-permute-start | bytes 2359304 | tf_op jit(solution)/shard_map/ppermute | solution.py:27
Sparse Core Ops, SparseCore 0:
  9.7 59.2 all-gather.1
where the time goes:
time: 218 us; the launch traced here: 217 us
  waiting for transfers between devices  134 us (61%)
  matrix products  31.9 us (15%)
  starting transfers between devices  26.8 us (12%)
  between operations  13.4 us (6%)
  other arithmetic  9.49 us (4%)
    all_gather x1, waiting for transfers between devices, per_device(): kernel = lax.all_gather(conv_weight, ('dp', 'seq'), axis=2, tiled=True)[0]  61.8 us
    ppermute x6, waiting for transfers between devices, from_behind(): return lax.ppermute(block, axis, route)  51.2 us
    dot_general x20, matrix products, convolve(): jnp.dot(padded[tap:tap + rows], kernel[tap], preferred_element_type=jnp.f...  31.9 us
    ppermute x5, waiting for transfers between devices, extended(): lax.ppermute(tail, axis, [(i, (i + 1) % count) for i in range(ends)])  20.7 us
    ppermute x5, starting transfers between devices, extended(): lax.ppermute(head, axis, [((i + 1) % count, i) for i in range(ends)])  12.6 us
    ppermute x6, starting transfers between devices, from_behind(): return lax.ppermute(block, axis, route)  7.75 us
    ppermute x5, starting transfers between devices, extended(): lax.ppermute(tail, axis, [(i, (i + 1) % count) for i in range(ends)])  6.46 us
    reduce_sum x5, other arithmetic, turn(): stat = jnp.mean(wide * wide, axis=-1, keepdims=True)  5.4 us
  transfers between devices with their start and end apart: 17, of which 12 were waited for; matrix products, arithmetic and copies ran while one was open for 1% of the time, Pallas kernels for 0%

commit v1 on v0

--- a/solution.py
+++ b/solution.py
@@ -1,7 +1,364 @@
+import functools
+
 import jax
 import jax.numpy as jnp
 from jax import lax
+from jax.experimental import pallas as pl
+from jax.experimental.pallas import tpu as pltpu
 from jax.sharding import PartitionSpec as P
+
+EDGE = 16
+HALF = 128
+WIDE = 256
+SIB, ACROSS, UP, DOWN = range(4)
+
+
+def column_chunks(width):
+    blocks = width // WIDE
+    chunks = [(0, 0, 0, HALF, True)]
+    for block in range(1, blocks):
+        chunks.append((block, 0, HALF + (block - 1) * WIDE, WIDE, False))
+    chunks.append((0, HALF, width - HALF, HALF, False))
+    return chunks
+
+
+def kernel(
+    seqs, act, weight, gain, bias, out,
+    xin, halo, wbuf, padded, shifted,
+    load_sem, own_sem, wsend, wrecv, hsend, hrecv, rsend, rrecv, esend, erecv,
+):
+    micros, rows, width = xin.shape
+    taps = weight.shape[1]
+    depth = weight.shape[2]
+    chunks = column_chunks(width)
+    dp = lax.axis_index("dp")
+    seg = lax.axis_index("segment")
+    z = lax.axis_index("seq")
+    chip, core = dp // 2, dp % 2
+    sib = chip * 2 + (1 - core)
+    across = (1 - chip) * 2 + core
+    has_up = z + 1 < seqs
+    has_down = z > 0
+    first = seg == 0
+
+    def always(body):
+        body()
+
+    def when(*conds):
+        conds = [c for c in conds if c is not None]
+        if not conds:
+            return always
+        return pl.when(functools.reduce(jnp.logical_and, conds))
+
+    targets = {
+        SIB: (None, (sib, seg, z)),
+        ACROSS: (None, (across, seg, z)),
+        UP: (has_up, (dp, seg, z + 1)),
+        DOWN: (has_down, (dp, seg, z - 1)),
+    }
+
+    barrier = pltpu.get_barrier_semaphore()
+
+    def greet(device):
+        pl.semaphore_signal(barrier, inc=1, device_id=device, device_id_type=pl.DeviceIdType.MESH)
+
+    greet((sib, seg, z))
+    greet((across, seg, z))
+    greet((dp, 1 - seg, z))
+
+    @pl.when(has_up)
+    def _():
+        greet((dp, seg, z + 1))
+        greet((dp, 1 - seg, z + 1))
+
+    @pl.when(has_down)
+    def _():
+        greet((dp, seg, z - 1))
+        greet((dp, 1 - seg, z - 1))
+
+    own_w = []
+    for j, (b, bc, c0, cw, _) in enumerate(chunks):
+        start = pl.multiple_of((dp * seqs + z) * depth, EDGE)
+        own_w.append(
+            pltpu.make_async_copy(
+                weight.at[0, :, :, pl.ds(c0, cw)],
+                wbuf.at[b, :, pl.ds(start, depth), pl.ds(bc, cw)],
+                own_sem.at[j],
+            )
+        )
+        own_w[-1].start()
+    load_x = pltpu.make_async_copy(act.at[0], xin, load_sem)
+
+    @pl.when(first)
+    def _():
+        load_x.start()
+
+    ends = jnp.int32(has_up) + jnp.int32(has_down)
+    pl.semaphore_wait(barrier, 3 + 2 * ends)
+
+    pending = []
+
+    def piece(j, owner, at):
+        b, bc, _, cw, _ = chunks[j]
+        start = pl.multiple_of((owner * seqs + at) * depth, EDGE)
+        return wbuf.at[b, :, pl.ds(start, depth), pl.ds(bc, cw)]
+
+    def transfer(j, owner, at, slot, way, own):
+        c0, cw = chunks[j][2:4]
+        dst = piece(j, owner, at)
+        return pltpu.make_async_remote_copy(
+            src_ref=weight.at[0, :, :, pl.ds(c0, cw)] if own else dst,
+            dst_ref=dst,
+            send_sem=wsend.at[j, slot * 4 + way],
+            recv_sem=wrecv.at[j, owner * seqs + at],
+            device_id=targets[way][1],
+            device_id_type=pl.DeviceIdType.MESH,
+        )
+
+    def spread(j, owner, at, slot, ways, own=False, cond=None):
+        for way in ways:
+            make = functools.partial(transfer, j, owner, at, slot, way, own)
+
+            @when(targets[way][0])
+            def _():
+                make().start()
+
+            pending.append((cond, targets[way][0], make))
+
+    def arrive(j, owner, at):
+        transfer(j, owner, at, 0, SIB, False).wait_recv()
+
+    def send_own(j):
+        spread(j, dp, z, z, (ACROSS, UP, DOWN, SIB), own=True)
+
+    def relay_weights(j):
+        x_first = chunks[j][4]
+        if x_first:
+            arrive(j, across, z)
+            spread(j, across, z, seqs + z, (UP, DOWN, SIB))
+        else:
+            arrive(j, across, z)
+            spread(j, across, z, seqs + z, (SIB,))
+        for d in range(1, seqs):
+            for there, way in ((z - d, UP), (z + d, DOWN)):
+                cond = there >= 0 if way == UP else there < seqs
+                other = seqs + there
+
+                @pl.when(cond)
+                def _():
+                    if x_first:
+                        arrive(j, dp, there)
+                        spread(j, dp, there, there, (way, SIB), cond=cond)
+                        arrive(j, across, there)
+                        spread(j, across, there, other, (way, SIB), cond=cond)
+                    else:
+                        arrive(j, dp, there)
+                        spread(j, dp, there, there, (way, ACROSS, SIB), cond=cond)
+
+            if not x_first:
+                for there, cond in ((z - d, z - d >= 0), (z + d, z + d < seqs)):
+                    other = seqs + there
+
+                    @pl.when(cond)
+                    def _():
+                        arrive(j, across, there)
+                        spread(j, across, there, other, (SIB,), cond=cond)
+
+    def from_sibling(j):
+        for at in range(seqs):
+            arrive(j, sib, at)
+            arrive(j, (1 - chip) * 2 + (1 - core), at)
+
+    def edge_in(side):
+        up = side == 0
+        return pltpu.make_async_remote_copy(
+            src_ref=act.at[0, :, pl.ds(rows - EDGE if up else 0, EDGE), :],
+            dst_ref=halo.at[side],
+            send_sem=hsend.at[side],
+            recv_sem=hrecv.at[side],
+            device_id=(dp, seg, z + 1 if up else z - 1),
+            device_id_type=pl.DeviceIdType.MESH,
+        )
+
+    def edge_out(j, side):
+        up = side == 0
+        cols = pl.ds(chunks[j][2], chunks[j][3])
+        return pltpu.make_async_remote_copy(
+            src_ref=out.at[0, 0, :, pl.ds(rows - EDGE if up else 0, EDGE), cols],
+            dst_ref=halo.at[side, :, :, cols],
+            send_sem=esend.at[j, side],
+            recv_sem=erecv.at[j, side],
+            device_id=(dp, 1 - seg, z + 1 if up else z - 1),
+            device_id_type=pl.DeviceIdType.MESH,
+        )
+
+    def rows_out(j):
+        cols = pl.ds(chunks[j][2], chunks[j][3])
+        return pltpu.make_async_remote_copy(
+            src_ref=out.at[0, 0, :, :, cols],
+            dst_ref=xin.at[:, :, cols],
+            send_sem=rsend.at[j],
+            recv_sem=rrecv.at[j],
+            device_id=(dp, 1 - seg, z),
+            device_id_type=pl.DeviceIdType.MESH,
+        )
+
+    for side, cond in ((0, z == 0), (1, z == seqs - 1)):
+
+        @pl.when(cond)
+        def _():
+            halo[side] = jnp.zeros(halo.shape[1:], halo.dtype)
+
+    def normed(cells):
+        wide = cells.astype(jnp.float32)
+        stat = jnp.mean(wide * wide, axis=-1, keepdims=True)
+        return wide * lax.rsqrt(stat + 1e-06) * gain[...]
+
+    def shift_rows():
+        def one(m, carry):
+            padded[m, pl.ds(0, EDGE)] = normed(halo[0, m])
+            padded[m, pl.ds(EDGE, rows)] = normed(xin[m])
+            padded[m, pl.ds(EDGE + rows, EDGE)] = normed(halo[1, m])
+            at = pl.multiple_of(m * rows, rows)
+            for tap in range(taps):
+                shifted[pl.ds(at, rows), pl.ds(tap * width, width)] = padded[
+                    m, pl.ds(EDGE - taps // 2 + tap, rows), :
+                ].astype(jnp.bfloat16)
+            return carry
+
+        lax.fori_loop(0, micros, one, 0)
+
+    def convolve(b, bc, cw):
+        kern = wbuf[b, :, :, pl.ds(bc, cw)].reshape(taps * width, cw)
+        return jnp.dot(shifted[...], kern, preferred_element_type=jnp.float32)
+
+    def finish(total, c0, cw, join):
+        cols = pl.ds(c0, cw)
+        wide = xin[:, :, cols].astype(jnp.float32)
+        total = total.reshape(micros, rows, cw) + bias[:, cols].reshape(1, 1, cw)
+        lifted = wide + jax.nn.gelu(total, approximate=True)
+        if join:
+            lifted = lifted + wide
+        out[0, 0, :, :, cols] = lifted.astype(out.dtype)
+
+    send_own(0)
+
+    @pl.when(first)
+    def _():
+        for side, cond in ((0, has_up), (1, has_down)):
+
+            @pl.when(cond)
+            def _():
+                edge_in(side).start()
+
+    send_own(1)
+
+    @pl.when(first)
+    def _():
+        load_x.wait()
+        for side, cond in ((0, has_down), (1, has_up)):
+
+            @pl.when(cond)
+            def _():
+                edge_in(side).wait_recv()
+
+        shift_rows()
+
+    for copy in own_w:
+        copy.wait()
+    for j, (b, bc, c0, cw, _) in enumerate(chunks):
+        relay_weights(j)
+        if j + 2 < len(chunks):
+            send_own(j + 2)
+        from_sibling(j)
+
+        @pl.when(first)
+        def _():
+            finish(convolve(b, bc, cw), c0, cw, False)
+            rows_out(j).start()
+            for side, cond in ((0, has_up), (1, has_down)):
+
+                @pl.when(cond)
+                def _():
+                    edge_out(j, side).start()
+
+    for outer, inner, make in pending:
+
+        @when(outer, inner)
+        def _():
+            make().wait_send()
+
+    @pl.when(first)
+    def _():
+        for side, cond in ((0, has_up), (1, has_down)):
+
+            @pl.when(cond)
+            def _():
+                edge_in(side).wait_send()
+                for j in range(len(chunks)):
+                    edge_out(j, side).wait_send()
+
+        for j in range(len(chunks)):
+            rows_out(j).wait_send()
+
+    @pl.when(jnp.logical_not(first))
+    def _():
+        for j in range(len(chunks)):
+            rows_out(j).wait_recv()
+        for side, cond in ((0, has_down), (1, has_up)):
+
+            @pl.when(cond)
+            def _():
+                for j in range(len(chunks)):
+                    edge_out(j, side).wait_recv()
+
+        shift_rows()
+        for b in range(width // WIDE):
+            total = convolve(b, 0, WIDE)
+            for block, bc, c0, cw, _ in chunks:
+                if block == b:
+                    finish(total[:, bc : bc + cw], c0, cw, True)
+
+
+def in_kernel(activations, conv_weight, norm_gain, conv_bias):
+    _, micros, rows, width = activations.shape
+    taps, depth = conv_weight.shape[1:3]
+    seqs = lax.axis_size("seq")
+    shards = lax.axis_size("dp") * seqs
+    count = len(column_chunks(width))
+    dma = pltpu.SemaphoreType.DMA
+    vmem = pl.BlockSpec(memory_space=pltpu.VMEM)
+    anywhere = pl.BlockSpec(memory_space=pl.ANY)
+    flops = 2 * micros * rows * taps * width * width
+    return pl.pallas_call(
+        functools.partial(kernel, seqs),
+        out_shape=jax.ShapeDtypeStruct((1, 1, micros, rows, width), jnp.bfloat16),
+        in_specs=[anywhere, anywhere, vmem, vmem],
+        out_specs=vmem,
+        scratch_shapes=[
+            pltpu.VMEM((micros, rows, width), jnp.bfloat16),
+            pltpu.VMEM((2, micros, EDGE, width), jnp.bfloat16),
+            pltpu.VMEM((width // WIDE, taps, width, WIDE), jnp.bfloat16),
+            pltpu.VMEM((micros, rows + 2 * EDGE, width), jnp.float32),
+            pltpu.VMEM((micros * rows, taps * width), jnp.bfloat16),
+            dma,
+            dma((count,)),
+            dma((count, 8 * seqs)),
+            dma((count, shards)),
+            dma((2,)),
+            dma((2,)),
+            dma((count,)),
+            dma((count,)),
+            dma((count, 2)),
+            dma((count, 2)),
+        ],
+        cost_estimate=pl.CostEstimate(
+            flops=flops, bytes_accessed=4 * activations.size, transcendentals=micros * rows * width
+        ),
+        compiler_params=pltpu.CompilerParams(
+            collective_id=0, has_side_effects=True, vmem_limit_bytes=48 * 1024 * 1024
+        ),
+    )(activations, conv_weight, norm_gain, conv_bias)
 
 
 def extended(cells, sides, width):
@@ -27,7 +384,7 @@
     return lax.ppermute(block, axis, route)
 
 
-def per_device(activations, conv_weight, norm_gain, conv_bias):
+def relayed(activations, conv_weight, norm_gain, conv_bias):
     kernel = lax.all_gather(conv_weight, ("dp", "seq"), axis=2, tiled=True)[0]
     gain = norm_gain[0]
     bias = conv_bias[0]
@@ -83,6 +440,16 @@
     return output[None, None]
 
 
+def per_device(activations, conv_weight, norm_gain, conv_bias):
+    _, _, rows, width = activations.shape
+    depth = conv_weight.shape[2]
+    two_blocks = lax.axis_size("segment") == 2 and lax.axis_size("dp") == 4
+    tiled = depth % EDGE == 0 and rows % EDGE == 0 and width % WIDE == 0
+    fits = two_blocks and tiled and conv_weight.shape[1] // 2 <= EDGE and width > WIDE
+    body = in_kernel if fits and lax.axis_size("seq") > 1 else relayed
+    return body(activations, conv_weight, norm_gain, conv_bias)
+
+
 def solution(mesh):
     in_specs = (
         P("dp", None, "seq", None),

time: 218 us -> 81.5 us (0.37)
  the two profiles are of different devices: /device:TPU:28 before, /device:TPU:5 now
where the time goes in v1:
time: 81.5 us; the launch traced here: 81.3 us
  Pallas kernels  76.9 us (94%)
  local copies, waits for them, and re-layouts  4.37 us (5%)
    pallas_call x1, Pallas kernels, in_kernel(): pl.pallas_call(functools.partial(kernel, seqs), out_shape=jax.ShapeDtypeS...  76.9 us
    unnamed x9, local copies, waits for them, and re-layouts  4.37 us

profile of v1, /device:TPU:5, one launch (start us, length us, event | category | flops | bytes accessed | tf_op | source)
XLA Modules:
  0.0 81.3 jit_solution(507461685749508196)
XLA Ops:
  0.0 0.0 copy-start
  0.0 1.1 %copy-done = bf16[1,4,128,768]{3,2,1,0:T(8,128)(2,1)S(1)} copy-done((bf16[1,4,128,768]{3,2,1,0:T(8,128)(2,1)S(1)}, bf16[1,4,128,768]{3,2,1,0:T(8,128)(2,1)}, u32[]{:S(2)}) %copy-start) | copy-done | bytes 786456
  1.1 0.0 copy-start.1
  1.1 1.0 %copy-done.1 = bf16[1,5,48,768]{3,2,1,0:T(8,128)(2,1)S(1)} copy-done((bf16[1,5,48,768]{3,2,1,0:T(8,128)(2,1)S(1)}, bf16[1,5,48,768]{3,2,1,0:T(8,128)(2,1)}, u32[]{:S(2)}) %copy-start.1) | copy-done | bytes 368664
  2.1 0.0 copy-start.2
  2.1 0.7 copy-done.2
  2.8 0.0 copy-start.3
  2.8 0.7 copy-done.3
  3.5 76.9 %shard_map.46 = bf16[1,1,4,128,768]{4,3,2,1,0:T(8,128)(2,1)S(1)} custom-call(bf16[1,4,128,768]{3,2,1,0:T(8,128)(2,1)S(1)} %copy-done, bf16[1,5,48,768]{3,2,1,0:T(8,128)(2,1)S(1)} %copy-done.1, f32[1,768]{1,0:T(1,128)S(1)} %copy-done.2, f32[1,768]{1,0:T(1,128)S(1)} %copy-done.3), custom_call_target="tpu_custom_call" | custom-call | flops 3019898880 | bytes 1572864 | tf_op jit(solution)/shard_map/pallas_call | solution.py:333
  80.4 0.9 %copy.6 = bf16[1,1,4,128,768]{4,3,2,1,0:T(8,128)(2,1)} copy(bf16[1,1,4,128,768]{4,3,2,1,0:T(8,128)(2,1)S(1)} %shard_map.46) | data formatting | bytes 1572864
Async XLA Ops:
  0.0 1.1 %copy-start = (bf16[1,4,128,768]{3,2,1,0:T(8,128)(2,1)S(1)}, bf16[1,4,128,768]{3,2,1,0:T(8,128)(2,1)}, u32[]{:S(2)}) copy-start(bf16[1,4,128,768]{3,2,1,0:T(8,128)(2,1)} %act.1) | copy-start | bytes 2359300
  1.1 1.0 %copy-start.1 = (bf16[1,5,48,768]{3,2,1,0:T(8,128)(2,1)S(1)}, bf16[1,5,48,768]{3,2,1,0:T(8,128)(2,1)}, u32[]{:S(2)}) copy-start(bf16[1,5,48,768]{3,2,1,0:T(8,128)(2,1)} %weight.1) | copy-start | bytes 1105924
  2.1 0.7 copy-start.2
  2.8 0.7 copy-start.3

commit v2 on v1

--- a/solution.py
+++ b/solution.py
@@ -10,22 +10,16 @@
 EDGE = 16
 HALF = 128
 WIDE = 256
-SIB, ACROSS, UP, DOWN = range(4)
 
 
 def column_chunks(width):
-    blocks = width // WIDE
-    chunks = [(0, 0, 0, HALF, True)]
-    for block in range(1, blocks):
-        chunks.append((block, 0, HALF + (block - 1) * WIDE, WIDE, False))
-    chunks.append((0, HALF, width - HALF, HALF, False))
-    return chunks
+    return [(c // WIDE, c % WIDE, c, HALF) for c in range(0, width, HALF)]
 
 
 def kernel(
-    seqs, act, weight, gain, bias, out,
-    xin, halo, wbuf, padded, shifted,
-    load_sem, own_sem, wsend, wrecv, hsend, hrecv, rsend, rrecv, esend, erecv,
+    seqs, act, weight, gain_in, bias_in, out,
+    gain, bias, xin, halo, wbuf, padded, shifted,
+    load_sem, gain_sem, bias_sem, own_sem, wsend, wrecv, hsend, hrecv, rsend, rrecv, esend, erecv,
 ):
     micros, rows, width = xin.shape
     taps = weight.shape[1]
@@ -41,21 +35,8 @@
     has_down = z > 0
     first = seg == 0
 
-    def always(body):
-        body()
-
-    def when(*conds):
-        conds = [c for c in conds if c is not None]
-        if not conds:
-            return always
-        return pl.when(functools.reduce(jnp.logical_and, conds))
-
-    targets = {
-        SIB: (None, (sib, seg, z)),
-        ACROSS: (None, (across, seg, z)),
-        UP: (has_up, (dp, seg, z + 1)),
-        DOWN: (has_down, (dp, seg, z - 1)),
-    }
+    ring = [lax.rem(z + d, seqs) for d in range(seqs)]
+    ways = seqs + 1
 
     barrier = pltpu.get_barrier_semaphore()
 
@@ -65,19 +46,19 @@
     greet((sib, seg, z))
     greet((across, seg, z))
     greet((dp, 1 - seg, z))
+    for at in ring[1:]:
+        greet((dp, seg, at))
 
     @pl.when(has_up)
     def _():
-        greet((dp, seg, z + 1))
         greet((dp, 1 - seg, z + 1))
 
     @pl.when(has_down)
     def _():
-        greet((dp, seg, z - 1))
         greet((dp, 1 - seg, z - 1))
 
     own_w = []
-    for j, (b, bc, c0, cw, _) in enumerate(chunks):
+    for j, (b, bc, c0, cw) in enumerate(chunks):
         start = pl.multiple_of((dp * seqs + z) * depth, EDGE)
         own_w.append(
             pltpu.make_async_copy(
@@ -88,85 +69,69 @@
         )
         own_w[-1].start()
     load_x = pltpu.make_async_copy(act.at[0], xin, load_sem)
+    load_gain = pltpu.make_async_copy(gain_in, gain, gain_sem)
+    load_bias = pltpu.make_async_copy(bias_in, bias, bias_sem)
+    load_gain.start()
+    load_bias.start()
 
     @pl.when(first)
     def _():
         load_x.start()
 
     ends = jnp.int32(has_up) + jnp.int32(has_down)
-    pl.semaphore_wait(barrier, 3 + 2 * ends)
+    pl.semaphore_wait(barrier, 2 + seqs + ends)
 
     pending = []
 
     def piece(j, owner, at):
-        b, bc, _, cw, _ = chunks[j]
+        b, bc, _, cw = chunks[j]
         start = pl.multiple_of((owner * seqs + at) * depth, EDGE)
         return wbuf.at[b, :, pl.ds(start, depth), pl.ds(bc, cw)]
 
     def transfer(j, owner, at, slot, way, own):
         c0, cw = chunks[j][2:4]
         dst = piece(j, owner, at)
+        if way == 0:
+            device = (sib, seg, z)
+        elif way == 1:
+            device = (across, seg, z)
+        else:
+            device = (dp, seg, ring[way - 1])
         return pltpu.make_async_remote_copy(
             src_ref=weight.at[0, :, :, pl.ds(c0, cw)] if own else dst,
             dst_ref=dst,
-            send_sem=wsend.at[j, slot * 4 + way],
+            send_sem=wsend.at[j, slot * ways + way],
             recv_sem=wrecv.at[j, owner * seqs + at],
-            device_id=targets[way][1],
+            device_id=device,
             device_id_type=pl.DeviceIdType.MESH,
         )
 
-    def spread(j, owner, at, slot, ways, own=False, cond=None):
-        for way in ways:
-            make = functools.partial(transfer, j, owner, at, slot, way, own)
-
-            @when(targets[way][0])
-            def _():
-                make().start()
-
-            pending.append((cond, targets[way][0], make))
+    def send(*piece_and_way):
+        transfer(*piece_and_way).start()
+        pending.append(piece_and_way)
 
     def arrive(j, owner, at):
-        transfer(j, owner, at, 0, SIB, False).wait_recv()
+        transfer(j, owner, at, 0, 0, False).wait_recv()
 
     def send_own(j):
-        spread(j, dp, z, z, (ACROSS, UP, DOWN, SIB), own=True)
-
-    def relay_weights(j):
-        x_first = chunks[j][4]
-        if x_first:
-            arrive(j, across, z)
-            spread(j, across, z, seqs + z, (UP, DOWN, SIB))
-        else:
-            arrive(j, across, z)
-            spread(j, across, z, seqs + z, (SIB,))
+        for way in [*range(2, ways), 1, 0]:
+            send(j, dp, z, 0, way, True)
+
+    def from_column(j):
         for d in range(1, seqs):
-            for there, way in ((z - d, UP), (z + d, DOWN)):
-                cond = there >= 0 if way == UP else there < seqs
-                other = seqs + there
-
-                @pl.when(cond)
-                def _():
-                    if x_first:
-                        arrive(j, dp, there)
-                        spread(j, dp, there, there, (way, SIB), cond=cond)
-                        arrive(j, across, there)
-                        spread(j, across, there, other, (way, SIB), cond=cond)
-                    else:
-                        arrive(j, dp, there)
-                        spread(j, dp, there, there, (way, ACROSS, SIB), cond=cond)
-
-            if not x_first:
-                for there, cond in ((z - d, z - d >= 0), (z + d, z + d < seqs)):
-                    other = seqs + there
-
-                    @pl.when(cond)
-                    def _():
-                        arrive(j, across, there)
-                        spread(j, across, there, other, (SIB,), cond=cond)
+            arrive(j, dp, ring[d])
+            send(j, dp, ring[d], d, 1, False)
+            send(j, dp, ring[d], d, 0, False)
+
+    def from_across(j):
+        for d in range(seqs):
+            arrive(j, across, ring[d])
+            send(j, across, ring[d], seqs + d, 0, False)
 
     def from_sibling(j):
-        for at in range(seqs):
+        for at in ring:
             arrive(j, sib, at)
+        for at in ring:
             arrive(j, (1 - chip) * 2 + (1 - core), at)
 
     def edge_in(side):
@@ -241,35 +206,9 @@
             lifted = lifted + wide
         out[0, 0, :, :, cols] = lifted.astype(out.dtype)
 
-    send_own(0)
-
-    @pl.when(first)
-    def _():
-        for side, cond in ((0, has_up), (1, has_down)):
-
-            @pl.when(cond)
-            def _():
-                edge_in(side).start()
-
-    send_own(1)
-
-    @pl.when(first)
-    def _():
-        load_x.wait()
-        for side, cond in ((0, has_down), (1, has_up)):
-
-            @pl.when(cond)
-            def _():
-                edge_in(side).wait_recv()
-
-        shift_rows()
-
-    for copy in own_w:
-        copy.wait()
-    for j, (b, bc, c0, cw, _) in enumerate(chunks):
-        relay_weights(j)
-        if j + 2 < len(chunks):
-            send_own(j + 2)
+    def complete(j):
+        b, bc, c0, cw = chunks[j]
+        from_across(j)
         from_sibling(j)
 
         @pl.when(first)
@@ -282,11 +221,40 @@
                 def _():
                     edge_out(j, side).start()
 
-    for outer, inner, make in pending:
-
-        @when(outer, inner)
-        def _():
-            make().wait_send()
+    @pl.when(first)
+    def _():
+        for side, cond in ((0, has_up), (1, has_down)):
+
+            @pl.when(cond)
+            def _():
+                edge_in(side).start()
+
+    for j in range(len(chunks)):
+        send_own(j)
+    load_gain.wait()
+    load_bias.wait()
+
+    @pl.when(first)
+    def _():
+        load_x.wait()
+        for side, cond in ((0, has_down), (1, has_up)):
+
+            @pl.when(cond)
+            def _():
+                edge_in(side).wait_recv()
+
+        shift_rows()
+
+    for copy in own_w:
+        copy.wait()
+    for j in range(len(chunks)):
+        from_column(j)
+        if j > 0:
+            complete(j - 1)
+    complete(len(chunks) - 1)
+
+    for piece_and_way in pending:
+        transfer(*piece_and_way).wait_send()
 
     @pl.when(first)
     def _():
@@ -315,7 +283,7 @@
         shift_rows()
         for b in range(width // WIDE):
             total = convolve(b, 0, WIDE)
-            for block, bc, c0, cw, _ in chunks:
+            for block, bc, c0, cw in chunks:
                 if block == b:
                     finish(total[:, bc : bc + cw], c0, cw, True)
 
@@ -333,17 +301,21 @@
     return pl.pallas_call(
         functools.partial(kernel, seqs),
         out_shape=jax.ShapeDtypeStruct((1, 1, micros, rows, width), jnp.bfloat16),
-        in_specs=[anywhere, anywhere, vmem, vmem],
+        in_specs=[anywhere] * 4,
         out_specs=vmem,
         scratch_shapes=[
+            pltpu.VMEM((1, width), jnp.float32),
+            pltpu.VMEM((1, width), jnp.float32),
             pltpu.VMEM((micros, rows, width), jnp.bfloat16),
             pltpu.VMEM((2, micros, EDGE, width), jnp.bfloat16),
             pltpu.VMEM((width // WIDE, taps, width, WIDE), jnp.bfloat16),
             pltpu.VMEM((micros, rows + 2 * EDGE, width), jnp.float32),
             pltpu.VMEM((micros * rows, taps * width), jnp.bfloat16),
             dma,
+            dma,
+            dma,
             dma((count,)),
-            dma((count, 8 * seqs)),
+            dma((count, 2 * seqs * (seqs + 1))),
             dma((count, shards)),
             dma((2,)),
             dma((2,)),
@@ -356,7 +328,7 @@
             flops=flops, bytes_accessed=4 * activations.size, transcendentals=micros * rows * width
         ),
         compiler_params=pltpu.CompilerParams(
-            collective_id=0, has_side_effects=True, vmem_limit_bytes=48 * 1024 * 1024
+            collective_id=0, has_side_effects=True, vmem_limit_bytes=60 * 1024 * 1024
         ),
     )(activations, conv_weight, norm_gain, conv_bias)
 

time: 81.5 us -> 67.3 us (0.83)
  Pallas kernels: 76.9 us -> 64.4 us
  local copies, waits for them, and re-layouts: 4.37 us -> 2.06 us
    pallas_call x1, Pallas kernels: 76.9 us -> 64.4 us  [in_kernel(): pl.pallas_call(functools.partial(kernel, seqs), out_shape=jax.ShapeDtypeS...]
    unnamed x9 -> x1, local copies, waits for them, and re-layouts: 4.37 us -> 2.06 us
where the time goes in v2:
time: 67.3 us; the launch traced here: 66.4 us
  Pallas kernels  64.4 us (96%)
  local copies, waits for them, and re-layouts  2.06 us (3%)
    pallas_call x1, Pallas kernels, in_kernel(): pl.pallas_call(functools.partial(kernel, seqs), out_shape=jax.ShapeDtypeS...  64.4 us
    unnamed x1, local copies, waits for them, and re-layouts  2.06 us

profile of v2, /device:TPU:5, one launch (start us, length us, event | category | flops | bytes accessed | tf_op | source)
XLA Modules:
  0.0 66.4 jit_solution(8201056173156800085)
XLA Ops:
  0.0 64.4 %shard_map.46 = bf16[1,1,4,128,768]{4,3,2,1,0:T(8,128)(2,1)} custom-call(bf16[1,4,128,768]{3,2,1,0:T(8,128)(2,1)} %act.1, bf16[1,5,48,768]{3,2,1,0:T(8,128)(2,1)} %weight.1, f32[1,768]{1,0:T(1,128)} %gain_in.1, f32[1,768]{1,0:T(1,128)} %bias_in.1), custom_call_target="tpu_custom_call" | custom-call | flops 3019898880 | bytes 1572864 | tf_op jit(solution)/shard_map/pallas_call | solution.py:301
  64.4 2.1 %copy.6 = bf16[1,1,4,128,768]{4,3,2,1,0:T(8,128)(2,1)} copy(bf16[1,1,4,128,768]{4,3,2,1,0:T(8,128)(2,1)} %shard_map.46) | data formatting | bytes 1572864

commit v3 on v2

--- a/solution.py
+++ b/solution.py
@@ -10,10 +10,6 @@
 EDGE = 16
 HALF = 128
 WIDE = 256
-
-
-def column_chunks(width):
-    return [(c // WIDE, c % WIDE, c, HALF) for c in range(0, width, HALF)]
 
 
 def kernel(
@@ -23,8 +19,7 @@
 ):
     micros, rows, width = xin.shape
     taps = weight.shape[1]
-    depth = weight.shape[2]
-    chunks = column_chunks(width)
+    count = width // HALF
     dp = lax.axis_index("dp")
     seg = lax.axis_index("segment")
     z = lax.axis_index("seq")
@@ -57,14 +52,14 @@
     def _():
         greet((dp, 1 - seg, z - 1))
 
+    def piece(j, owner, at):
+        return wbuf.at[j, owner * seqs + at]
+
     own_w = []
-    for j, (b, bc, c0, cw) in enumerate(chunks):
-        start = pl.multiple_of((dp * seqs + z) * depth, EDGE)
+    for j in range(count):
         own_w.append(
             pltpu.make_async_copy(
-                weight.at[0, :, :, pl.ds(c0, cw)],
-                wbuf.at[b, :, pl.ds(start, depth), pl.ds(bc, cw)],
-                own_sem.at[j],
+                weight.at[0, :, :, pl.ds(j * HALF, HALF)], piece(j, dp, z), own_sem.at[j]
             )
         )
         own_w[-1].start()
@@ -83,14 +78,8 @@
 
     pending = []
 
-    def piece(j, owner, at):
-        b, bc, _, cw = chunks[j]
-        start = pl.multiple_of((owner * seqs + at) * depth, EDGE)
-        return wbuf.at[b, :, pl.ds(start, depth), pl.ds(bc, cw)]
-
-    def transfer(j, owner, at, slot, way, own):
-        c0, cw = chunks[j][2:4]
-        dst = piece(j, owner, at)
+    def transfer(j, owner, at, slot, way):
+        block = piece(j, owner, at)
         if way == 0:
             device = (sib, seg, z)
         elif way == 1:
@@ -98,8 +87,8 @@
         else:
             device = (dp, seg, ring[way - 1])
         return pltpu.make_async_remote_copy(
-            src_ref=weight.at[0, :, :, pl.ds(c0, cw)] if own else dst,
-            dst_ref=dst,
+            src_ref=block,
+            dst_ref=block,
             send_sem=wsend.at[j, slot * ways + way],
             recv_sem=wrecv.at[j, owner * seqs + at],
             device_id=device,
@@ -111,22 +100,22 @@
         pending.append(piece_and_way)
 
     def arrive(j, owner, at):
-        transfer(j, owner, at, 0, 0, False).wait_recv()
+        transfer(j, owner, at, 0, 0).wait_recv()
 
     def send_own(j):
         for way in [*range(2, ways), 1, 0]:
-            send(j, dp, z, 0, way, True)
+            send(j, dp, z, 0, way)
 
     def from_column(j):
         for d in range(1, seqs):
             arrive(j, dp, ring[d])
-            send(j, dp, ring[d], d, 1, False)
-            send(j, dp, ring[d], d, 0, False)
+            send(j, dp, ring[d], d, 1)
+            send(j, dp, ring[d], d, 0)
 
     def from_across(j):
         for d in range(seqs):
             arrive(j, across, ring[d])
-            send(j, across, ring[d], seqs + d, 0, False)
+            send(j, across, ring[d], seqs + d, 0)
 
     def from_sibling(j):
         for at in ring:
@@ -147,7 +136,7 @@
 
     def edge_out(j, side):
         up = side == 0
-        cols = pl.ds(chunks[j][2], chunks[j][3])
+        cols = pl.ds(j * HALF, HALF)
         return pltpu.make_async_remote_copy(
             src_ref=out.at[0, 0, :, pl.ds(rows - EDGE if up else 0, EDGE), cols],
             dst_ref=halo.at[side, :, :, cols],
@@ -158,7 +147,7 @@
         )
 
     def rows_out(j):
-        cols = pl.ds(chunks[j][2], chunks[j][3])
+        cols = pl.ds(j * HALF, HALF)
         return pltpu.make_async_remote_copy(
             src_ref=out.at[0, 0, :, :, cols],
             dst_ref=xin.at[:, :, cols],
@@ -193,8 +182,14 @@
 
         lax.fori_loop(0, micros, one, 0)
 
-    def convolve(b, bc, cw):
-        kern = wbuf[b, :, :, pl.ds(bc, cw)].reshape(taps * width, cw)
+    def convolve(*parts):
+        kern = jnp.concatenate(
+            [
+                jnp.concatenate([wbuf[j, :, tap].reshape(width, HALF) for j in parts], axis=1)
+                for tap in range(taps)
+            ],
+            axis=0,
+        )
         return jnp.dot(shifted[...], kern, preferred_element_type=jnp.float32)
 
     def finish(total, c0, cw, join):
@@ -207,13 +202,12 @@
         out[0, 0, :, :, cols] = lifted.astype(out.dtype)
 
     def complete(j):
-        b, bc, c0, cw = chunks[j]
         from_across(j)
         from_sibling(j)
 
         @pl.when(first)
         def _():
-            finish(convolve(b, bc, cw), c0, cw, False)
+            finish(convolve(j), j * HALF, HALF, False)
             rows_out(j).start()
             for side, cond in ((0, has_up), (1, has_down)):
 
@@ -229,7 +223,8 @@
             def _():
                 edge_in(side).start()
 
-    for j in range(len(chunks)):
+    for j in range(count):
+        own_w[j].wait()
         send_own(j)
     load_gain.wait()
     load_bias.wait()
@@ -245,13 +240,11 @@
 
         shift_rows()
 
-    for copy in own_w:
-        copy.wait()
-    for j in range(len(chunks)):
+    for j in range(count):
         from_column(j)
         if j > 0:
             complete(j - 1)
-    complete(len(chunks) - 1)
+    complete(count - 1)
 
     for piece_and_way in pending:
         transfer(*piece_and_way).wait_send()
@@ -263,29 +256,26 @@
             @pl.when(cond)
             def _():
                 edge_in(side).wait_send()
-                for j in range(len(chunks)):
+                for j in range(count):
                     edge_out(j, side).wait_send()
 
-        for j in range(len(chunks)):
+        for j in range(count):
             rows_out(j).wait_send()
 
     @pl.when(jnp.logical_not(first))
     def _():
-        for j in range(len(chunks)):
+        for j in range(count):
             rows_out(j).wait_recv()
         for side, cond in ((0, has_down), (1, has_up)):
 
             @pl.when(cond)
             def _():
-                for j in range(len(chunks)):
+                for j in range(count):
                     edge_out(j, side).wait_recv()
 
         shift_rows()
-        for b in range(width // WIDE):
-            total = convolve(b, 0, WIDE)
-            for block, bc, c0, cw in chunks:
-                if block == b:
-                    finish(total[:, bc : bc + cw], c0, cw, True)
+        for j in range(0, count, 2):
+            finish(convolve(j, j + 1), j * HALF, WIDE, True)
 
 
 def in_kernel(activations, conv_weight, norm_gain, conv_bias):
@@ -293,7 +283,7 @@
     taps, depth = conv_weight.shape[1:3]
     seqs = lax.axis_size("seq")
     shards = lax.axis_size("dp") * seqs
-    count = len(column_chunks(width))
+    count = width // HALF
     dma = pltpu.SemaphoreType.DMA
     vmem = pl.BlockSpec(memory_space=pltpu.VMEM)
     anywhere = pl.BlockSpec(memory_space=pl.ANY)
@@ -308,7 +298,7 @@
             pltpu.VMEM((1, width), jnp.float32),
             pltpu.VMEM((micros, rows, width), jnp.bfloat16),
             pltpu.VMEM((2, micros, EDGE, width), jnp.bfloat16),
-            pltpu.VMEM((width // WIDE, taps, width, WIDE), jnp.bfloat16),
+            pltpu.VMEM((count, shards, taps, depth, HALF), jnp.bfloat16),
             pltpu.VMEM((micros, rows + 2 * EDGE, width), jnp.float32),
             pltpu.VMEM((micros * rows, taps * width), jnp.bfloat16),
             dma,

time: 67.3 us -> 67.2 us (level)
  no operation moved by 1% of the time
where the time goes in v3:
time: 67.2 us; the launch traced here: 66.4 us
  Pallas kernels  64.3 us (96%)
  local copies, waits for them, and re-layouts  2.06 us (3%)
    pallas_call x1, Pallas kernels, in_kernel(): pl.pallas_call(functools.partial(kernel, seqs), out_shape=jax.ShapeDtypeS...  64.3 us
    unnamed x1, local copies, waits for them, and re-layouts  2.06 us

profile of v3, /device:TPU:5, one launch (start us, length us, event | category | flops | bytes accessed | tf_op | source)
XLA Modules:
  0.0 66.4 jit_solution(3303921467789377397)
XLA Ops:
  0.0 64.3 %shard_map.46 = bf16[1,1,4,128,768]{4,3,2,1,0:T(8,128)(2,1)} custom-call(bf16[1,4,128,768]{3,2,1,0:T(8,128)(2,1)} %act.1, bf16[1,5,48,768]{3,2,1,0:T(8,128)(2,1)} %weight.1, f32[1,768]{1,0:T(1,128)} %gain_in.1, f32[1,768]{1,0:T(1,128)} %bias_in.1), custom_call_target="tpu_custom_call" | custom-call | flops 3019898880 | bytes 1572864 | tf_op jit(solution)/shard_map/pallas_call | solution.py:291
  64.3 2.1 %copy.6 = bf16[1,1,4,128,768]{4,3,2,1,0:T(8,128)(2,1)} copy(bf16[1,1,4,128,768]{4,3,2,1,0:T(8,128)(2,1)} %shard_map.46) | data formatting | bytes 1572864

commit v4 on v3

--- a/solution.py
+++ b/solution.py
@@ -31,7 +31,7 @@
     first = seg == 0
 
     ring = [lax.rem(z + d, seqs) for d in range(seqs)]
-    ways = seqs + 1
+    ways = seqs + 2
 
     barrier = pltpu.get_barrier_semaphore()
 
@@ -78,14 +78,14 @@
 
     pending = []
 
-    def transfer(j, owner, at, slot, way):
+    def transfer(j, owner, at, slot, way, to=None):
         block = piece(j, owner, at)
         if way == 0:
             device = (sib, seg, z)
         elif way == 1:
             device = (across, seg, z)
         else:
-            device = (dp, seg, ring[way - 1])
+            device = (dp, seg, to)
         return pltpu.make_async_remote_copy(
             src_ref=block,
             dst_ref=block,
@@ -95,27 +95,55 @@
             device_id_type=pl.DeviceIdType.MESH,
         )
 
-    def send(*piece_and_way):
-        transfer(*piece_and_way).start()
-        pending.append(piece_and_way)
+    def send(cond, *transfer_args):
+        if cond is None:
+            transfer(*transfer_args).start()
+        else:
+
+            @pl.when(cond)
+            def _():
+                transfer(*transfer_args).start()
+
+        pending.append((cond, transfer_args))
 
     def arrive(j, owner, at):
         transfer(j, owner, at, 0, 0).wait_recv()
 
+    last = seqs - 1
+    near = [jnp.logical_or(t == z + 1, t == z - 1) for t in ring]
+    direct = [
+        jnp.logical_or(near[d], jnp.logical_and(ring[d] > 0, ring[d] < last)) for d in range(seqs)
+    ]
+    to_first = [jnp.logical_and(z == 1, t > z) for t in ring]
+    to_last = [jnp.logical_and(z == last - 1, t < z) for t in ring]
+    partner = z + 1 - 2 * (z % 2)
+    not_partner = [t != partner for t in ring]
+
+    def by_partner(j):
+        return seqs % 2 == 0 and j % 2 == 0
+
     def send_own(j):
-        for way in [*range(2, ways), 1, 0]:
-            send(j, dp, z, 0, way)
+        for d in range(1, seqs):
+            send(direct[d], j, dp, z, 0, 1 + d, ring[d])
+        send(None, j, dp, z, 0, 1)
+        send(None, j, dp, z, 0, 0)
 
     def from_column(j):
+        arrive(j, across, z)
+        if by_partner(j):
+            send(None, j, across, z, seqs, 2, partner)
+        send(None, j, across, z, seqs, 0)
+        for d in [1, *range(seqs - 1, 1, -1)]:
+            arrive(j, dp, ring[d])
+            send(to_first[d], j, dp, ring[d], d, 2, z - 1)
+            send(to_last[d], j, dp, ring[d], d, 3, z + 1)
+            send(not_partner[d] if by_partner(j) else None, j, dp, ring[d], d, 1)
+            send(None, j, dp, ring[d], d, 0)
+
+    def from_across(j):
         for d in range(1, seqs):
-            arrive(j, dp, ring[d])
-            send(j, dp, ring[d], d, 1)
-            send(j, dp, ring[d], d, 0)
-
-    def from_across(j):
-        for d in range(seqs):
             arrive(j, across, ring[d])
-            send(j, across, ring[d], seqs + d, 0)
+            send(None, j, across, ring[d], seqs + d, 0)
 
     def from_sibling(j):
         for at in ring:
@@ -246,8 +274,14 @@
             complete(j - 1)
     complete(count - 1)
 
-    for piece_and_way in pending:
-        transfer(*piece_and_way).wait_send()
+    for cond, transfer_args in pending:
+        if cond is None:
+            transfer(*transfer_args).wait_send()
+        else:
+
+            @pl.when(cond)
+            def _():
+                transfer(*transfer_args).wait_send()
 
     @pl.when(first)
     def _():
@@ -305,7 +339,7 @@
             dma,
             dma,
             dma((count,)),
-            dma((count, 2 * seqs * (seqs + 1))),
+            dma((count, 2 * seqs * (seqs + 2))),
             dma((count, shards)),
             dma((2,)),
             dma((2,)),

time: 67.2 us -> 68.6 us (1.021)
  Pallas kernels: 64.3 us -> 66.4 us
    pallas_call x1, Pallas kernels: 64.3 us -> 66.4 us  [in_kernel(): pl.pallas_call(functools.partial(kernel, seqs), out_shape=jax.ShapeDtypeS...]
where the time goes in v4:
time: 68.6 us; the launch traced here: 68.4 us
  Pallas kernels  66.4 us (97%)
  local copies, waits for them, and re-layouts  2.06 us (3%)
    pallas_call x1, Pallas kernels, in_kernel(): pl.pallas_call(functools.partial(kernel, seqs), out_shape=jax.ShapeDtypeS...  66.4 us
    unnamed x1, local copies, waits for them, and re-layouts  2.06 us

profile of v4, /device:TPU:5, one launch (start us, length us, event | category | flops | bytes accessed | tf_op | source)
XLA Modules:
  0.0 68.4 jit_solution(10245126116294935279)
XLA Ops:
  0.0 66.4 %shard_map.46 = bf16[1,1,4,128,768]{4,3,2,1,0:T(8,128)(2,1)} custom-call(bf16[1,4,128,768]{3,2,1,0:T(8,128)(2,1)} %act.1, bf16[1,5,48,768]{3,2,1,0:T(8,128)(2,1)} %weight.1, f32[1,768]{1,0:T(1,128)} %gain_in.1, f32[1,768]{1,0:T(1,128)} %bias_in.1), custom_call_target="tpu_custom_call" | custom-call | flops 3019898880 | bytes 1572864 | tf_op jit(solution)/shard_map/pallas_call | solution.py:325
  66.4 2.1 %copy.6 = bf16[1,1,4,128,768]{4,3,2,1,0:T(8,128)(2,1)} copy(bf16[1,1,4,128,768]{4,3,2,1,0:T(8,128)(2,1)} %shard_map.46) | data formatting | bytes 1572864

commit v5 on v3

--- a/solution.py
+++ b/solution.py
@@ -103,7 +103,7 @@
         transfer(j, owner, at, 0, 0).wait_recv()
 
     def send_own(j):
-        for way in [*range(2, ways), 1, 0]:
+        for way in [1, *range(2, ways), 0]:
             send(j, dp, z, 0, way)
 
     def from_column(j):
@@ -223,7 +223,7 @@
             def _():
                 edge_in(side).start()
 
-    for j in range(count):
+    for j in range(2):
         own_w[j].wait()
         send_own(j)
     load_gain.wait()
@@ -242,6 +242,9 @@
 
     for j in range(count):
         from_column(j)
+        if j + 2 < count:
+            own_w[j + 2].wait()
+            send_own(j + 2)
         if j > 0:
             complete(j - 1)
     complete(count - 1)

time: 67.2 us -> 66.3 us (0.987)
  the two profiles are of different devices: /device:TPU:5 before, /device:TPU:13 now
where the time goes in v5:
time: 66.3 us; the launch traced here: 66.1 us
  Pallas kernels  64.1 us (97%)
  local copies, waits for them, and re-layouts  2.06 us (3%)
    pallas_call x1, Pallas kernels, in_kernel(): pl.pallas_call(functools.partial(kernel, seqs), out_shape=jax.ShapeDtypeS...  64.1 us
    unnamed x1, local copies, waits for them, and re-layouts  2.06 us

profile of v5, /device:TPU:13, one launch (start us, length us, event | category | flops | bytes accessed | tf_op | source)
XLA Modules:
  0.0 66.1 jit_solution(6976827255567414792)
XLA Ops:
  0.0 64.1 %shard_map.46 = bf16[1,1,4,128,768]{4,3,2,1,0:T(8,128)(2,1)} custom-call(bf16[1,4,128,768]{3,2,1,0:T(8,128)(2,1)} %act.1, bf16[1,5,48,768]{3,2,1,0:T(8,128)(2,1)} %weight.1, f32[1,768]{1,0:T(1,128)} %gain_in.1, f32[1,768]{1,0:T(1,128)} %bias_in.1), custom_call_target="tpu_custom_call" | custom-call | flops 3019898880 | bytes 1572864 | tf_op jit(solution)/shard_map/pallas_call | solution.py:294
  64.1 2.1 %copy.6 = bf16[1,1,4,128,768]{4,3,2,1,0:T(8,128)(2,1)} copy(bf16[1,1,4,128,768]{4,3,2,1,0:T(8,128)(2,1)} %shard_map.46) | data formatting | bytes 1572864
